TPU v7x, 32 devices: a whole 2x2x4 slice. The times are simulated.
32 devices in a mesh: parts: 2 (over y), people: 4 (over z), markers: 4 (over x, core).
Axes of the slice: x: 2, y: 2, z: 4, core: 2. Of those that a mesh axis runs over, the one named last changes fastest.
Arguments:
- dosages: float32 [4096, 8192], P(('parts', 'people'), 'markers'), parts along dimension 0, may hold values from 0 to 2
- freq: float32 [16384], P(('parts', 'markers')), parts along dimension 0, may hold values from 0.05 to 0.5
- pair_cols: int32 [8, 4], P(('parts', 'people')), parts along dimension 0, may hold values from 0 to 3, as said below
- pair_count: int32 [8], P(('parts', 'people')), parts along dimension 0, may hold values from 1 to 4, as said below
Outputs:
- tiles: float32 [512, 32, 512], P('markers', ('parts', 'people')), parts along dimension 1
There are 2 independent parts, one for each index of `parts`. A program takes and returns all parts, laid end to end along the dimension named above; each array names one. Nothing has to cross between parts.
Inputs may be any that keep to these rules, and one draw needn't show every extreme that they name: `pair_cols`: entry 0 of row r is r itself; every entry of row r is (r + k) mod 4 for some k from 0 to 7. Some row block r lists (r + min(s, 7)) mod 4 in slot s for every s, with all 4 tiles live. `pair_count`: some row block has all 4 listed tiles live.
All inputs are finite; a program needn't handle non-finite values.
Results may differ from a plain program's by a relative error of at most 0.0003.
Values may be sent and summed in bfloat16 or wider, within the bound.
A program may use at most 128 MiB of HBM per device.

v0:
```python
import jax
import jax.numpy as jnp
from jax import lax
from jax.sharding import PartitionSpec as P

MARKERS = 8192


def standardize(dosages, freq):
    doubled_freq = 2.0 * freq
    spread = jnp.sqrt(doubled_freq * (1.0 - freq))
    return ((dosages - doubled_freq) / spread).astype(jnp.bfloat16)


def on_device(dosages, freq, pair_cols, pair_count):
    standard = standardize(dosages, freq)
    listed_cols = pair_cols[0]
    gathered = lax.all_gather(standard, "people", axis=0, tiled=True)
    sources = gathered.reshape(-1, standard.shape[0], standard.shape[1])
    slot_total = listed_cols.shape[0]
    live_count = pair_count[0]
    columns = jnp.take(sources, listed_cols, axis=0)
    partial_value = (
        jnp.einsum("im,sjm->isj", standard, columns, preferred_element_type=jnp.float32) / MARKERS
    )
    live_mask = (jnp.arange(slot_total, dtype=jnp.int32) < live_count).astype(jnp.float32)
    partial_value = partial_value * live_mask[None, :, None]
    return lax.psum_scatter(partial_value, "markers", scatter_dimension=0, tiled=True)


def solution(mesh):
    in_specs = (
        P(("parts", "people"), "markers"),
        P(("parts", "markers")),
        P(("parts", "people"), None),
        P(("parts", "people")),
    )
    out_specs = P("markers", ("parts", "people"), None)
    return jax.shard_map(
        on_device, mesh=mesh, in_specs=in_specs, out_specs=out_specs, check_vma=False
    )
```

profile of v0, /device:TPU:0, one launch (start us, length us, event | category | flops | bytes accessed | tf_op | source)
XLA Modules:
  0.0 242.5 jit_solution(10378952044234829412)
XLA Ops:
  6.5 0.0 all-gather.2.cloned.1.call-start
  6.5 0.7 broadcast_multiply_fusion.1
  7.2 0.0 copy-start.1
  7.2 4.1 %divide_convert_fusion = bf16[512,2048]{1,0:T(8,128)(2,1)} fusion(f32[512,2048]{1,0:T(8,128)} %param.4, f32[2048]{0:T(1024)S(1)} %get-tuple-element.8, f32[2048]{0:T(1024)S(1)} %get-tuple-element.7), kind=kLoop, calls=%fused_computation.8 | loop fusion | flops 3145728 | bytes 6307840 | tf_op jit(solution)/shard_map/convert_element_type | solution.py:12
  11.4 0.0 all-gather.2.cloned.1.call-update
  11.4 0.0 reduce-scatter.2.cloned.1.call-start
  12.1 0.0 copy-done.1
  12.2 151.7 %all-gather.2.cloned.1.call-done = bf16[2048,2048]{1,0:T(8,128)(2,1)} async-done(((bf16[512,2048]{1,0:T(8,128)(2,1)}), bf16[2048,2048]{1,0:T(8,128)(2,1)}) %all-gather.2.cloned.1.call-update) | async-done | bytes 8388624 | tf_op jit(solution)/shard_map/all_gather | solution.py:18
  163.9 5.9 %fusion.11 = (bf16[4,512,1024]{2,1,0:T(8,128)(2,1)}, bf16[4,512,1024]{2,1,0:T(8,128)(2,1)}) fusion(bf16[4,512,2048]{2,1,0:T(8,128)(2,1)} %bitcast.14), kind=kLoop, calls=%fused_computation.21 | loop fusion | bytes 16777216 | tf_op jit(solution)/shard_map/jit(_take)/gather | solution.py:22
  169.8 4.9 %gather_fusion = bf16[4,512,1024]{2,1,0:T(8,128)(2,1)} fusion(bf16[4,512,1024]{2,1,0:T(8,128)(2,1)} %get-tuple-element.5, s32[1024]{0:T(1024)S(1)} %pad_clamp_fusion), kind=kCustom, calls=%fused_computation | custom fusion | bytes 8388624 | tf_op jit(solution)/shard_map/jit(_take)/gather | solution.py:22
  174.7 0.0 copy-start
  174.7 5.1 %gather_fusion.1 = bf16[4,512,1024]{2,1,0:T(8,128)(2,1)} fusion(bf16[4,512,1024]{2,1,0:T(8,128)(2,1)} %get-tuple-element.6, s32[1024]{0:T(1024)S(1)} %pad_clamp_fusion), kind=kCustom, calls=%fused_computation.1 | custom fusion | bytes 8388624 | tf_op jit(solution)/shard_map/jit(_take)/gather | solution.py:22
  179.9 0.0 copy-done
  179.9 10.0 %broadcast_multiply_fusion = f32[512,4,512]{2,0,1:T(8,128)} fusion(f32[4]{0:T(128)S(1)} %compare_select_fusion.2, bf16[4,512,1024]{2,1,0:T(8,128)(2,1)} %gather_fusion.1, bf16[4,512,1024]{2,1,0:T(8,128)(2,1)} %gather_fusion, pred[4]{0:T(512)(128)(4,1)S(1)} %compare_and_fusion, bf16[512,2048]{1,0:T(8,128)(2,1)S(1)} %copy-done), kind=kOutput, calls=%fused_computation.10 | convolution fusion | flops 4316987392 | bytes 14680084 | tf_op jit(solution)/shard_map/im,sjm->isj/dot_general | solution.py:24
  189.9 0.0 reduce-scatter.2.cloned.1.call-update
  189.9 42.9 %reduce-scatter.2.cloned.1.call-done = f32[128,4,512]{2,0,1:T(8,128)} async-done(((f32[512,4,512]{2,0,1:T(8,128)}), f32[128,4,512]{2,0,1:T(8,128)}) %reduce-scatter.2.cloned.1.call-update) | async-done | bytes 1048592 | tf_op jit(solution)/shard_map/reduce_scatter | solution.py:28
  232.8 2.9 %copy.5 = f32[128,4,512]{2,1,0:T(4,128)} copy(f32[128,4,512]{2,0,1:T(8,128)} %reduce-scatter.2.cloned.1.call-done) | data formatting | bytes 2097152 | tf_op jit(solution)/shard_map/reduce_scatter | solution.py:28
  (4 shorter events, 0.0 us)
Async XLA Ops:
  6.5 157.4 %all-gather.2.cloned.1.call-start = ((), (), s32[]{:S(2)}) async-start(), calls=%async_computation.1 | async-start | bytes 10485760 | tf_op jit(solution)/shard_map/all_gather | solution.py:18
  7.2 4.9 %copy-start.1 = (s32[1,4]{1,0:T(1,128)S(1)}, s32[1,4]{1,0:T(1,128)}, u32[]{:S(2)}) copy-start(s32[1,4]{1,0:T(1,128)} %param.6) | copy-start | bytes 52
  11.4 221.4 %reduce-scatter.2.cloned.1.call-start = ((), (), s32[]{:S(2)}) async-start(), calls=%async_computation.2 | async-start | bytes 5242880 | tf_op jit(solution)/shard_map/reduce_scatter | solution.py:28
  174.7 5.1 %copy-start = (bf16[512,2048]{1,0:T(8,128)(2,1)S(1)}, bf16[512,2048]{1,0:T(8,128)(2,1)}, u32[]{:S(2)}) copy-start(bf16[512,2048]{1,0:T(8,128)(2,1)} %divide_convert_fusion) | copy-start | bytes 6291460
Sparse Core Ops, SparseCore 0:
  11.5 152.3 all-gather.1
  190.1 42.7 reduce-scatter.1
where the time goes:
time: 243 us
  waiting for transfers between devices  195 us (80%)
  local copies, waits for them, and re-layouts  18.9 us (8%)
  between operations  14.1 us (6%)
  matrix products  10 us (4%)
  other arithmetic  4.86 us (2%)
    all_gather x1, waiting for transfers between devices, on_device(): gathered = lax.all_gather(standard, 'people', axis=0, tiled=True)  152 us
    reduce_scatter x1, waiting for transfers between devices, on_device(): lax.psum_scatter(partial_value, 'markers', scatter_dimension=0, tiled=True)  42.9 us
    gather x3, local copies, waits for them, and re-layouts, on_device(): columns = jnp.take(sources, listed_cols, axis=0)  16 us
    dot_general x1, matrix products, on_device(): jnp.einsum('im,sjm->isj', standard, columns, preferred_element_type=jnp.f...  10 us
  transfers between devices with their start and end apart: 2, of which 2 were waited for; matrix products, arithmetic and copies ran while one was open for 0% of the time, Pallas kernels for 0%

commit v1 on v0

v1 whole, which is shorter than its diff:
```python
import functools

import jax
import jax.numpy as jnp
from jax import lax
from jax.experimental import pallas as pl
from jax.experimental.pallas import tpu as pltpu
from jax.sharding import PartitionSpec as P

MESH = pl.DeviceIdType.MESH
PIECES = 4


def standardize(dosages, freq):
    doubled_freq = 2.0 * freq
    spread = jnp.sqrt(doubled_freq * (1.0 - freq))
    return ((dosages - doubled_freq) / spread).astype(jnp.bfloat16)


def gather_all(markers, dosages, freq, pair_cols, pair_count):
    standard = standardize(dosages, freq)
    listed_cols = pair_cols[0]
    gathered = lax.all_gather(standard, "people", axis=0, tiled=True)
    sources = gathered.reshape(-1, standard.shape[0], standard.shape[1])
    slot_total = listed_cols.shape[0]
    live_count = pair_count[0]
    columns = jnp.take(sources, listed_cols, axis=0)
    partial_value = (
        jnp.einsum("im,sjm->isj", standard, columns, preferred_element_type=jnp.float32) / markers
    )
    live_mask = (jnp.arange(slot_total, dtype=jnp.int32) < live_count).astype(jnp.float32)
    partial_value = partial_value * live_mask[None, :, None]
    return lax.psum_scatter(partial_value, "markers", scatter_dimension=0, tiled=True)


OWN, OUT, OPP, FAR = range(4)


def make_jobs(tile):
    half, piece = tile // 2, tile // PIECES
    early = [(0, OWN, 0, tile), (0, OPP, 0, half), (0, OPP, half, half)]
    middle = [(1, OWN, 0, tile), (1, OUT, 0, tile), (0, OUT, 0, tile), (1, OPP, 0, tile)]
    late = [(b, FAR, k * piece, piece) for k in range(PIECES) for b in (1, 0)]
    return early, middle, late


def kernel(scale, dos_ref, freq_ref, out_ref, std, got, acc, crecv, xrecv, fin, ores,
           out_send, out_recv, opp_send, opp_recv, far_send, far_recv,
           c_send, c_recv, x_send, x_recv, r_send, r_recv):
    tile = std.shape[0]
    piece = tile // PIECES
    z = lax.axis_index("people")
    m = lax.axis_index("markers")
    x, c = m // 2, m % 2
    is_inner = jnp.logical_and(z >= 1, z <= 2)
    mate = z + 1 - 2 * (z % 2)
    opposite = 3 - z
    core_mate = 2 * x + 1 - c
    x_mate = 2 * (1 - x) + c

    barrier = pltpu.get_barrier_semaphore()

    def greet(**where):
        pl.semaphore_signal(barrier, inc=1, device_id=where, device_id_type=MESH)

    greet(people=mate)

    @pl.when(is_inner)
    def _():
        greet(people=opposite)
        greet(markers=core_mate)
        greet(markers=x_mate)

    def rows(k):
        return pl.ds(k * piece, piece)

    doubled = 2.0 * freq_ref[...]
    inverse = 1.0 / jnp.sqrt(doubled * (1.0 - freq_ref[...]))

    def fill(k):
        step = 16

        @pl.loop(0, piece // step)
        def _(t):
            at = pl.ds(pl.multiple_of(k * piece + t * step, step), step)
            std[at, :] = ((dos_ref[at, :] - doubled) * inverse).astype(jnp.bfloat16)

    def remote(src, dst, send, recv, **where):
        return pltpu.make_async_remote_copy(
            src_ref=src, dst_ref=dst, send_sem=send, recv_sem=recv,
            device_id=where, device_id_type=MESH)

    early, middle, late = make_jobs(tile)
    jobs = early + middle + late
    outward = [j for j, job in enumerate(jobs) if job[0] == 1]

    def to_mate(k):
        return remote(std.at[rows(k)], got.at[0, rows(k)], out_send.at[k], out_recv.at[k], people=mate)

    def to_opposite(k):
        return remote(std.at[rows(k)], got.at[1, rows(k)], opp_send.at[k], opp_recv.at[k], people=opposite)

    def forward(k):
        return remote(got.at[0, rows(k)], got.at[2, rows(k)], far_send.at[k], far_recv.at[k], people=opposite)

    def core_copy(j):
        b, col, lo, n = jobs[j]
        return remote(acc.at[b, col, :, 1 - c, :, pl.ds(lo, n)], crecv.at[b, col, :, :, pl.ds(lo, n)],
                      c_send.at[j], c_recv.at[j], markers=core_mate)

    def x_copy(j):
        b, col, lo, n = jobs[j]
        return remote(acc.at[b, col, 1 - x, c, :, pl.ds(lo, n)], xrecv.at[b, col, :, pl.ds(lo, n)],
                      x_send.at[j], x_recv.at[j], markers=x_mate)

    def result_copy(j):
        b, col, lo, n = jobs[j]
        return remote(fin.at[col, :, pl.ds(lo, n)], ores.at[col, :, pl.ds(lo, n)],
                      r_send.at[j], r_recv.at[j], people=mate)

    @pl.when(jnp.logical_not(is_inner))
    def _():
        fill(0)
        pl.semaphore_wait(barrier, 1)
        to_mate(0).start()
        for k in range(1, PIECES):
            fill(k)
            to_mate(k).start()
        for k in range(PIECES):
            to_mate(k).wait_send()
        for j in outward:
            _, col, lo, n = jobs[j]
            result_copy(j).wait_recv()
            out_ref[col, :, pl.ds(lo, n)] = ores[col, :, pl.ds(lo, n)]

    @pl.when(is_inner)
    def _():
        fill(0)
        pl.semaphore_wait(barrier, 4)
        to_opposite(0).start()
        for k in range(1, PIECES):
            fill(k)
            to_opposite(k).start()

        def compute(j):
            b, col, lo, n = jobs[j]
            height = tile // 4

            @pl.loop(0, 2)
            def _(h):
                left_rows = pl.ds(pl.multiple_of(h * 2 * height, 2 * height), 2 * height)
                left = std[left_rows, :] if b == 0 else got[0, left_rows, :]
                right = std[pl.ds(lo, n), :] if col == OWN else got[col - 1, pl.ds(lo, n), :]
                product = lax.dot_general(left, right, (((1,), (1,)), ((), ())),
                                          preferred_element_type=jnp.float32)
                acc[b, col, h, 0, :, pl.ds(lo, n)] = product[:height]
                acc[b, col, h, 1, :, pl.ds(lo, n)] = product[height:]
            core_copy(j).start()

        def add_core(j):
            b, col, lo, n = jobs[j]
            core_copy(j).wait_recv()
            at = pl.ds(lo, n)
            acc[b, col, 1 - x, c, :, at] += crecv[b, col, 1 - x, :, at]
            x_copy(j).start()
            acc[b, col, x, c, :, at] += crecv[b, col, x, :, at]

        def finish(j):
            b, col, lo, n = jobs[j]
            at = pl.ds(lo, n)
            x_copy(j).wait_recv()
            value = (acc[b, col, x, c, :, at] + xrecv[b, col, :, at]) * scale
            if b == 1:
                fin[col, :, at] = value
                result_copy(j).start()
            else:
                out_ref[col, :, at] = value

        def arrive(k):
            to_mate(k).wait_recv()
            forward(k).start()

        done = {"x": 0, "f": 0}

        def push_x(upto):
            while done["x"] < upto:
                add_core(done["x"])
                done["x"] += 1

        def push_f(upto):
            while done["f"] < upto:
                finish(done["f"])
                done["f"] += 1

        compute(0)
        arrive(0)
        push_x(1)
        arrive(1)
        to_opposite(0).wait_recv()
        to_opposite(1).wait_recv()
        compute(1)
        arrive(2)
        push_x(2)
        push_f(1)
        to_opposite(2).wait_recv()
        to_opposite(3).wait_recv()
        compute(2)
        arrive(3)
        push_x(3)
        for j in range(3, 7):
            compute(j)
            push_x(j)
            push_f(j - 2)
        push_x(7)
        for k in range(PIECES):
            forward(k).wait_recv()
            j = 7 + 2 * k
            compute(j)
            compute(j + 1)
            push_x(j + 2)
            push_f(j)
        push_f(len(jobs))
        for k in range(PIECES):
            to_opposite(k).wait_send()
            forward(k).wait_send()
        for j in range(len(jobs)):
            core_copy(j).wait_send()
            x_copy(j).wait_send()
        for j in outward:
            result_copy(j).wait_send()


def four_blocks(markers, dosages, freq, pair_cols, pair_count):
    tile, depth = dosages.shape
    height = tile // 4
    early, middle, late = make_jobs(tile)
    n_jobs = len(early + middle + late)
    dma = pltpu.SemaphoreType.DMA
    vmem = pl.BlockSpec(memory_space=pltpu.VMEM)
    by_name = pl.pallas_call(
        functools.partial(kernel, 1.0 / markers),
        out_shape=jax.ShapeDtypeStruct((4, height, tile), jnp.float32),
        in_specs=[vmem, vmem],
        out_specs=vmem,
        scratch_shapes=[
            pltpu.VMEM((tile, depth), jnp.bfloat16),
            pltpu.VMEM((3, tile, depth), jnp.bfloat16),
            pltpu.VMEM((2, 4, 2, 2, height, tile), jnp.float32),
            pltpu.VMEM((2, 4, 2, height, tile), jnp.float32),
            pltpu.VMEM((2, 4, height, tile), jnp.float32),
            pltpu.VMEM((4, height, tile), jnp.float32),
            pltpu.VMEM((4, height, tile), jnp.float32),
        ] + [dma((PIECES,))] * 6 + [dma((n_jobs,))] * 6,
        compiler_params=pltpu.CompilerParams(
            collective_id=0, has_side_effects=True, vmem_limit_bytes=52 * 2**20),
        cost_estimate=pl.CostEstimate(
            flops=2 * 2 * tile * 4 * tile * depth, bytes_accessed=6 * tile * depth, transcendentals=0),
    )(dosages, freq.reshape(1, depth))

    low = lax.axis_index("people") < 2
    names = jnp.where(low, jnp.array([OUT, OWN, OPP, FAR], jnp.int32), jnp.array([FAR, OPP, OWN, OUT], jnp.int32))
    slots = pair_cols.shape[1]
    tiles = []
    for s in range(slots):
        name = jnp.sum(jnp.where(jnp.arange(4, dtype=jnp.int32) == pair_cols[0, s], names, 0))
        live = s < pair_count[0]
        value = jnp.zeros_like(by_name[0])
        for k in range(4):
            value = jnp.where(jnp.logical_and(live, name == k), by_name[k], value)
        tiles.append(value)
    return jnp.stack(tiles, axis=1)


def solution(mesh):
    in_specs = (
        P(("parts", "people"), "markers"),
        P(("parts", "markers")),
        P(("parts", "people"), None),
        P(("parts", "people")),
    )
    out_specs = P("markers", ("parts", "people"), None)

    def on_device(dosages, *rest):
        markers = dosages.shape[1] * mesh.shape["markers"]
        four = mesh.shape["people"] == 4 and mesh.shape["markers"] == 4
        return (four_blocks if four else gather_all)(markers, dosages, *rest)

    return jax.shard_map(
        on_device, mesh=mesh, in_specs=in_specs, out_specs=out_specs, check_vma=False
    )
```

time: 243 us -> 127 us (0.52)
  waiting for transfers between devices: 195 us -> 0 us
  Pallas kernels: 0 us -> 108 us
  local copies, waits for them, and re-layouts: 18.9 us -> 3.8 us
  matrix products: 10 us -> 0 us
  between operations: 14.1 us -> 10.4 us
    all_gather x1 -> x0, waiting for transfers between devices: 152 us -> none  [on_device(): gathered = lax.all_gather(standard, 'people', axis=0, tiled=True)]
    pallas_call x0 -> x1, Pallas kernels: none -> 108 us  [four_blocks(): pl.pallas_call(functools.partial(kernel, 1.0 / markers), out_shape=jax.Sh...]
    reduce_scatter x1 -> x0, waiting for transfers between devices: 42.9 us -> none  [on_device(): lax.psum_scatter(partial_value, 'markers', scatter_dimension=0, tiled=True)]
    gather x3 -> x0, local copies, waits for them, and re-layouts: 16 us -> none  [on_device(): columns = jnp.take(sources, listed_cols, axis=0)]
    dot_general x1 -> x0, matrix products: 10 us -> none  [on_device(): jnp.einsum('im,sjm->isj', standard, columns, preferred_element_type=jnp.f...]
    convert_element_type x1 -> x0, other arithmetic: 4.14 us -> none  [standardize(): return ((dosages - doubled_freq) / spread).astype(jnp.bfloat16)]
    reduce_sum x0 -> x1, other arithmetic: none -> 3.89 us  [four_blocks(): jnp.sum(jnp.where(jnp.arange(4, dtype=jnp.int32) == pair_cols[0, s], name...]
    reduce_scatter x1 -> x0, local copies, waits for them, and re-layouts: 2.87 us -> none  [on_device(): lax.psum_scatter(partial_value, 'markers', scatter_dimension=0, tiled=True)]
  transfers between devices with their start and end apart: 2 -> 0, of which waited for: 2 -> 0; matrix products, arithmetic and copies ran while one was open for 0% -> 0% of each run, Pallas kernels for 0% -> 0%
where the time goes in v1:
time: 127 us
  Pallas kernels  108 us (85%)
  between operations  10.4 us (8%)
  other arithmetic  4.18 us (3%)
  local copies, waits for them, and re-layouts  3.8 us (3%)
    pallas_call x1, Pallas kernels, four_blocks(): pl.pallas_call(functools.partial(kernel, 1.0 / markers), out_shape=jax.Sh...  108 us
    reduce_sum x1, other arithmetic, four_blocks(): jnp.sum(jnp.where(jnp.arange(4, dtype=jnp.int32) == pair_cols[0, s], name...  3.89 us

profile of v1, /device:TPU:0, one launch (start us, length us, event | category | flops | bytes accessed | tf_op | source)
XLA Modules:
  0.0 126.5 jit_solution(9334008884259548753)
XLA Ops:
  0.0 1.5 %fusion.4 = (s32[1,1]{1,0:T(1,128)}, s32[1,1]{1,0:T(1,128)}, s32[1,1]{1,0:T(1,128)}, s32[1,1]{1,0:T(1,128)}) fusion(s32[1,4]{1,0:T(1,128)} %param.8), kind=kLoop, calls=%fused_computation.14 | loop fusion | bytes 32 | tf_op jit(solution)/shard_map/slice | solution.py:265
  1.5 3.9 %fusion = (s32[]{:T(128)}, s32[]{:T(128)}, s32[]{:T(128)}, s32[]{:T(128)}) fusion(s32[]{:T(128)} %bitcast.1, s32[4]{0:T(128)} %constant.27.clone, s32[4]{0:T(128)} %constant.28.clone, pred[]{:T(512)S(6)} %lt.3, s32[]{:T(128)} %bitcast.5, s32[]{:T(128)} %bitcast.8, s32[]{:T(128)} %bitcast.11), kind=kLoop, calls=%fused_computation.10 | loop fusion | flops 48 | bytes 65 | tf_op jit(solution)/shard_map/reduce_sum | solution.py:265
  11.0 0.0 copy-start
  11.0 0.7 copy-done
  11.7 108.1 %shard_map.64 = f32[4,128,512]{2,1,0:T(8,128)S(1)} custom-call(f32[512,2048]{1,0:T(8,128)} %dos_ref.1, f32[1,2048]{1,0:T(1,128)S(1)} %bitcast.17), custom_call_target="tpu_custom_call" | custom-call | flops 8589934592 | bytes 6291456 | tf_op jit(solution)/shard_map/pallas_call | solution.py:240
  119.8 0.1 select_bitcast_fusion.3
  124.7 0.1 select_bitcast_fusion.1
  124.8 0.1 pad_maximum_fusion
  124.9 1.6 %copy.7 = f32[128,4,512]{2,1,0:T(4,128)} copy(f32[128,4,512]{2,0,1:T(8,128)S(1)} %pad_maximum_fusion) | data formatting | bytes 2097152 | tf_op jit(solution)/shard_map/stack | solution.py:271
Async XLA Ops:
  11.0 0.7 copy-start
